TPU v7x, 512 devices: a whole 4x4x16 slice. The times are simulated.
512 devices in a mesh: leaf: 512 (over y, x, z, core).
Axes of the slice: x: 4, y: 4, z: 16, core: 2. Of those that a mesh axis runs over, the one named last changes fastest.
Arguments:
- densities: float32 [16, 524288], P(None, 'leaf'), may hold values from -6 to 6
- points: float32 [3, 524288], P(None, 'leaf'), may hold values from 0 to 1
- area_normals: float32 [3, 524288], P(None, 'leaf'), may hold values from -0.234375 to 0.234375
- col_basis: float32 [64, 524288], P(None, 'leaf'), may hold values from -0.375 to 0.375
- row_basis: float32 [64, 524288], P(None, 'leaf'), may hold values from -0.75 to 0.75
- up_leaf: float32 [2048, 4096], P('leaf'), may hold values from -0.5 to 0.5
- up_mid: float32 [1024, 4096], P('leaf'), may hold values from -0.5 to 0.5
- down_leaf: float32 [2048, 4096], P('leaf'), may hold values from -0.5 to 0.5
- down_mid: float32 [1024, 4096], P('leaf'), may hold values from -0.5 to 0.5
- couple_leaf: float32 [2048, 6, 4096], P('leaf'), may hold values from -0.3125 to 0.3125
- couple_mid: float32 [1024, 6, 4096], P('leaf'), may hold values from -0.3125 to 0.3125
- couple_top: float32 [512, 16, 4096], P('leaf'), may hold values from -0.1875 to 0.1875
- near_list: int32 [2048, 8], P('leaf'), may hold values from 0 to 2047, as said below
- near_count: int32 [2048], P('leaf'), may hold values from 1 to 8
- adm_leaf: int32 [2048, 6], P('leaf'), may hold values from 0 to 2047, as said below
- adm_mid: int32 [1024, 6], P('leaf'), may hold values from 0 to 1023, as said below
- adm_top: int32 [512, 16], P('leaf'), may hold values from 0 to 511
Outputs:
- potential: float32 [16, 524288], P(None, 'leaf')
Inputs may be any that keep to these rules, and one draw needn't show every extreme that they name: `near_list`: entry 0 of each row is the leaf itself; every other entry lies within 4 leaves of it. `adm_leaf`: every source lies in the leaf range of the device just before or just after the one that holds the target leaf. `adm_mid`: every source lies among the middle-level clusters of the device just before or just after the one that holds the target.
All inputs are finite; a program needn't handle non-finite values.
Results may differ from a plain program's by a relative error of at most 0.0003.
Values sent between devices are 32-bit elements; how exact they have to be, the bound alone decides.
No kernel may reach another device: no remote copies, remote signals or barrier semaphores. Data moves between devices by JAX's collectives and lax.ppermute only.
A program may use at most 64 MiB of HBM per device.

v0:
```python
import math
import jax
import jax.numpy as jnp
from jax import lax
from jax.sharding import PartitionSpec as P

RHS = 16
LEAF = 256
RANK = 64
NEAR = 8
ADM_LEAF = 6
ADM_MID = 6
ADM_TOP = 16
smooth_sq = 0.01
four_pi = 4.0 * math.pi
highest = lax.Precision.HIGHEST


def with_halo(block, sides, width):
    for axis, dim in sides:
        count = lax.axis_size(axis)
        forward = [(i, i + 1) for i in range(count - 1)]
        backward = [(target, source) for source, target in forward]
        low = lax.ppermute(
            lax.slice_in_dim(block, block.shape[dim] - width, None, axis=dim), axis, forward
        )
        high = lax.ppermute(lax.slice_in_dim(block, 0, width, axis=dim), axis, backward)
        block = jnp.concatenate([low, block, high], axis=dim)
    return block


def kernel_block(target, source, normals):
    delta_x = target[0][None, :] - source[0][:, None]
    delta_y = target[1][None, :] - source[1][:, None]
    delta_z = target[2][None, :] - source[2][:, None]
    radius_sq = delta_x * delta_x + delta_y * delta_y + delta_z * delta_z + smooth_sq
    along = (
        normals[0][:, None] * delta_x
        + normals[1][:, None] * delta_y
        + normals[2][:, None] * delta_z
    )
    return along / (four_pi * radius_sq * jnp.sqrt(radius_sq))


def coefficients(dens_rows, basis_rows, cluster_count):
    return jnp.einsum(
        "rlp,klp->lrk",
        dens_rows.reshape(RHS, cluster_count, LEAF),
        basis_rows.reshape(RANK, cluster_count, LEAF),
        precision=highest,
    )


def climb(children, transfers):
    groups = transfers.shape[0]
    return jnp.einsum(
        "mcrk,mckj->mrj", children.reshape(groups, 2, RHS, RANK), transfers, precision=highest
    )


def descend(parents, transfers, coupled):
    groups = parents.shape[0]
    total = coupled.reshape(groups, 2, RHS, RANK) + jnp.einsum(
        "mrk,mckj->mcrj", parents, transfers, precision=highest
    )
    return total.reshape(groups * 2, RHS, RANK)


def couple(sources, blocks):
    return jnp.einsum("tark,takj->trj", sources, blocks, precision=highest)


def on_device(
    densities,
    points,
    area_normals,
    col_basis,
    row_basis,
    up_leaf,
    up_mid,
    down_leaf,
    down_mid,
    couple_leaf,
    couple_mid,
    couple_top,
    near_list,
    near_count,
    adm_leaf,
    adm_mid,
    adm_top,
):
    leaf_count = near_list.shape[0]
    mid_count = leaf_count // 2
    span_size = densities.shape[1]
    device_index = lax.axis_index("leaf")
    first_leaf = device_index * leaf_count
    stacked = jnp.concatenate([densities, points, area_normals], 0)
    widened = with_halo(stacked, (("leaf", 1),), span_size)
    own_leaf = coefficients(densities, col_basis, leaf_count)
    own_mid = climb(own_leaf, up_leaf.reshape(mid_count, 2, RANK, RANK))
    packed = jnp.concatenate(
        [own_leaf.reshape(leaf_count, RHS * RANK), own_mid.reshape(mid_count, RHS * RANK)], 0
    )
    rim_coefs = with_halo(packed, (("leaf", 0),), leaf_count + mid_count)
    rim_groups = rim_coefs.reshape(3, leaf_count + mid_count, RHS, RANK)
    wide_leaf = rim_groups[:, :leaf_count].reshape(3 * leaf_count, RHS, RANK)
    wide_mid = rim_groups[:, leaf_count:].reshape(3 * mid_count, RHS, RANK)
    wide_dens = widened[:RHS]
    wide_points = widened[RHS : RHS + 3]
    wide_normals = widened[RHS + 3 : RHS + 6]
    own_top = climb(own_mid, up_mid.reshape(1, 2, RANK, RANK))
    top_blocks = couple_top.reshape(1, ADM_TOP, RANK, RANK)
    every_top = lax.all_gather(own_top.reshape(1, RHS * RANK), "leaf", axis=0, tiled=True)
    chosen_top = jnp.take(every_top, adm_top[0], axis=0).reshape(1, ADM_TOP, RHS, RANK)
    top_field = couple(chosen_top, top_blocks)
    mid_base = device_index * mid_count - mid_count
    mid_sources = jnp.take(wide_mid, adm_mid - mid_base, axis=0)
    mid_couple = couple(mid_sources, couple_mid.reshape(mid_count, ADM_MID, RANK, RANK))
    mid_field = descend(top_field, down_mid.reshape(1, 2, RANK, RANK), mid_couple)
    leaf_base = first_leaf - leaf_count
    leaf_sources = jnp.take(wide_leaf, adm_leaf - leaf_base, axis=0)
    leaf_couple = couple(leaf_sources, couple_leaf.reshape(leaf_count, ADM_LEAF, RANK, RANK))
    leaf_field = descend(mid_field, down_leaf.reshape(mid_count, 2, RANK, RANK), leaf_couple)
    far_part = jnp.einsum(
        "lrk,klp->rlp", leaf_field, row_basis.reshape(RANK, leaf_count, LEAF), precision=highest
    ).reshape(RHS, span_size)

    def block_term(target, source_leaf):
        start = (source_leaf - leaf_base) * LEAF
        block = kernel_block(
            target,
            lax.dynamic_slice_in_dim(wide_points, start, LEAF, 1),
            lax.dynamic_slice_in_dim(wide_normals, start, LEAF, 1),
        )
        return jnp.dot(
            lax.dynamic_slice_in_dim(wide_dens, start, LEAF, 1), block, precision=highest
        )

    def one_leaf(item):
        local_leaf, sources, count = item
        target = lax.dynamic_slice_in_dim(points, local_leaf * LEAF, LEAF, 1)
        total = jnp.zeros((RHS, LEAF), jnp.float32)
        for slot_index in range(NEAR):
            term = block_term(target, sources[slot_index])
            total = total + jnp.where(slot_index < count, term, jnp.zeros_like(term))
        return total

    near_blocks = lax.map(
        one_leaf, (jnp.arange(leaf_count, dtype=jnp.int32), near_list, near_count)
    )
    near_part = jnp.transpose(near_blocks, (1, 0, 2)).reshape(RHS, span_size)
    return 0.5 * densities + near_part + far_part


def solution(mesh):
    return jax.shard_map(
        on_device,
        mesh=mesh,
        in_specs=(
            P(None, "leaf"),
            P(None, "leaf"),
            P(None, "leaf"),
            P(None, "leaf"),
            P(None, "leaf"),
            P("leaf", None),
            P("leaf", None),
            P("leaf", None),
            P("leaf", None),
            P("leaf", None, None),
            P("leaf", None, None),
            P("leaf", None, None),
            P("leaf", None),
            P("leaf"),
            P("leaf", None),
            P("leaf", None),
            P("leaf", None),
        ),
        out_specs=P(None, "leaf"),
        check_vma=False,
    )
```

profile of v0, /device:TPU:1, one launch (start us, length us, event | category | flops | bytes accessed | tf_op | source)
XLA Modules:
  0.0 237.5 jit_solution(17463821512557997660)
XLA Ops:
  6.6 1.0 reshape.249
  7.6 1.3 fusion.193
  9.4 8.8 %collective-permute-start.3 = (f32[6,1024]{1,0:T(8,128)S(1)}, f32[6,1024]{1,0:T(8,128)S(1)}, u32[]{:S(2)}, u32[]{:S(2)}) collective-permute-start(f32[6,1024]{1,0:T(8,128)S(1)} %pad_maximum_fusion.5), channel_id=1, source_target_pairs={{1,0},{2,1},{3,2},{4,3},{5,4},{6,5},{7,6},{8,7},{9,8},{10,9},{11,1... | collective-permute-start | bytes 73736 | tf_op jit(solution)/shard_map/ppermute | solution.py:27
  18.2 1.9 collective-permute-start.2
  20.1 0.9 pad_maximum_fusion.1
  21.0 2.4 %collective-permute-start.1 = (f32[22,1024]{1,0:T(8,128)S(1)}, f32[22,1024]{1,0:T(8,128)S(1)}, u32[]{:S(2)}, u32[]{:S(2)}) collective-permute-start(f32[22,1024]{1,0:T(8,128)S(1)} %pad_maximum_fusion.1), channel_id=1, source_target_pairs={{1,0},{2,1},{3,2},{4,3},{5,4},{6,5},{7,6},{8,7},{9,8},{10,9},{11,1... | collective-permute-start | bytes 270344 | tf_op jit(solution)/shard_map/ppermute | solution.py:27
  23.4 3.2 %collective-permute-start = (f32[22,1024]{1,0:T(8,128)S(1)}, f32[22,1024]{1,0:T(8,128)S(1)}, u32[]{:S(2)}, u32[]{:S(2)}) collective-permute-start(f32[22,1024]{1,0:T(8,128)S(1)} %pad_maximum_fusion.1), channel_id=1, source_target_pairs={{0,1},{1,2},{2,3},{3,4},{4,5},{5,6},{6,7},{7,8},{8,9},{9,10},{10,1... | collective-permute-start | bytes 270344 | tf_op jit(solution)/shard_map/ppermute | solution.py:24
  26.6 0.9 reshape.258
  27.7 0.7 reshape.295
  28.4 0.7 fusion.204
  29.0 0.7 compare_and_fusion
  29.7 0.7 compare_and_fusion.2
  30.5 0.7 compare_and_fusion.1
  31.3 1.4 reshape.253
  33.6 0.6 gather_fusion
  34.8 0.7 fusion.188
  36.1 73.6 %while.10 = (s32[]{:T(128)}, f32[4,16,256]{2,1,0:T(8,128)S(1)}, s32[4]{0:T(128)S(1)}, s32[4,8]{1,0:T(4,128)}, s32[]{:T(128)}, /*index=5*/f32[16,3072]{1,0:T(8,12...) while((s32[]{:T(128)}, f32[4,16,256]{2,1,0:T(8,128)S(1)}, ...), condition=%wide.region_1.2_spmd, body=%wide.region_0.1_spmd.sunk | while | flops 109637680 | bytes 556135 | solution.py:148
  36.1 0.7 constant_dynamic-slice_fusion.21
  36.8 0.7 fusion.260
  42.7 0.6 dynamic_slice.123
  44.2 0.6 dynamic_slice.124
  47.9 0.6 fusion.262
  53.9 0.6 fusion.267
  54.5 0.7 constant_dynamic-slice_fusion.21
  55.2 0.7 fusion.260
  61.1 0.6 dynamic_slice.123
  62.6 0.6 dynamic_slice.124
  72.3 0.6 fusion.267
  72.9 0.7 constant_dynamic-slice_fusion.21
  73.6 0.7 fusion.260
  79.6 0.6 dynamic_slice.123
  81.0 0.6 dynamic_slice.124
  84.7 0.6 fusion.262
  87.1 0.6 fusion.264
  89.5 0.6 fusion.266
  90.7 0.6 fusion.267
  91.3 0.7 constant_dynamic-slice_fusion.21
  92.0 0.7 fusion.260
  98.0 0.6 dynamic_slice.123
  99.4 0.6 dynamic_slice.124
  103.1 0.6 fusion.262
  105.5 0.6 fusion.264
  107.9 0.6 fusion.266
  109.1 0.6 fusion.267
  109.7 116.4 %all-gather.3.cloned.1.call-done = f32[512,1,1024]{2,1,0:T(1,128)} async-done(((f32[1,1,1024]{2,1,0:T(1,128)}), f32[512,1,1024]{2,1,0:T(1,128)}) %all-gather.3.cloned.1.call-update) | async-done | bytes 2097168 | tf_op jit(solution)/shard_map/all_gather | solution.py:113
  226.2 2.1 copy.67
  228.2 0.6 gather_fusion.2
  230.0 0.6 add_add_fusion
  (86 shorter events, 17.1 us)
Async XLA Ops:
  6.5 26.1 %copy-start.4 = (f32[2,6,4096]{2,0,1:T(2,128)S(1)}, f32[2,6,4096]{2,0,1:T(2,128)}, u32[]{:S(2)}) copy-start(f32[2,6,4096]{2,0,1:T(2,128)} %param.29) | copy-start | bytes 589828
  6.5 26.4 %copy-start.1 = (f32[1,16,4096]{2,1,0:T(8,128)S(1)}, f32[1,16,4096]{2,1,0:T(8,128)}, u32[]{:S(2)}) copy-start(f32[1,16,4096]{2,1,0:T(8,128)} %param.30) | copy-start | bytes 786436
  6.5 26.7 %copy-start.7 = (f32[2,4096]{1,0:T(2,128)S(1)}, f32[2,4096]{1,0:T(2,128)}, u32[]{:S(2)}) copy-start(f32[2,4096]{1,0:T(2,128)} %param.27) | copy-start | bytes 98308
  6.5 26.8 %copy-start.6 = (f32[4,4096]{1,0:T(4,128)S(1)}, f32[4,4096]{1,0:T(4,128)}, u32[]{:S(2)}) copy-start(f32[4,4096]{1,0:T(4,128)} %param.26) | copy-start | bytes 196612
  6.5 219.6 %all-gather.3.cloned.1.call-start = ((), (), s32[]{:S(2)}) async-start(), calls=%async_computation | async-start | bytes 2101248 | tf_op jit(solution)/shard_map/all_gather | solution.py:113
  9.4 24.1 %collective-permute-start.3 = (f32[6,1024]{1,0:T(8,128)S(1)}, f32[6,1024]{1,0:T(8,128)S(1)}, u32[]{:S(2)}, u32[]{:S(2)}) collective-permute-start(f32[6,1024]{1,0:T(8,128)S(1)} %pad_maximum_fusion.5), channel_id=1, source_target_pairs={{1,0},{2,1},{3,2},{4,3},{5,4},{6,5},{7,6},{8,7},{9,8},{10,9},{11,1... | collective-permute-start | bytes 73736 | tf_op jit(solution)/shard_map/ppermute | solution.py:27
  18.2 15.3 %collective-permute-start.2 = (f32[6,1024]{1,0:T(8,128)S(1)}, f32[6,1024]{1,0:T(8,128)S(1)}, u32[]{:S(2)}, u32[]{:S(2)}) collective-permute-start(f32[6,1024]{1,0:T(8,128)S(1)} %pad_maximum_fusion.5), channel_id=1, source_target_pairs={{0,1},{1,2},{2,3},{3,4},{4,5},{5,6},{6,7},{7,8},{8,9},{9,10},{10,1... | collective-permute-start | bytes 73736 | tf_op jit(solution)/shard_map/ppermute | solution.py:24
  21.0 14.9 %collective-permute-start.1 = (f32[22,1024]{1,0:T(8,128)S(1)}, f32[22,1024]{1,0:T(8,128)S(1)}, u32[]{:S(2)}, u32[]{:S(2)}) collective-permute-start(f32[22,1024]{1,0:T(8,128)S(1)} %pad_maximum_fusion.1), channel_id=1, source_target_pairs={{1,0},{2,1},{3,2},{4,3},{5,4},{6,5},{7,6},{8,7},{9,8},{10,9},{11,1... | collective-permute-start | bytes 270344 | tf_op jit(solution)/shard_map/ppermute | solution.py:27
  23.4 12.5 %collective-permute-start = (f32[22,1024]{1,0:T(8,128)S(1)}, f32[22,1024]{1,0:T(8,128)S(1)}, u32[]{:S(2)}, u32[]{:S(2)}) collective-permute-start(f32[22,1024]{1,0:T(8,128)S(1)} %pad_maximum_fusion.1), channel_id=1, source_target_pairs={{0,1},{1,2},{2,3},{3,4},{4,5},{5,6},{6,7},{7,8},{8,9},{9,10},{10,1... | collective-permute-start | bytes 270344 | tf_op jit(solution)/shard_map/ppermute | solution.py:24
  33.0 3.0 %copy-start = (f32[16,1024]{1,0:T(8,128)S(1)}, f32[16,1024]{1,0:T(8,128)}, u32[]{:S(2)}) copy-start(f32[16,1024]{1,0:T(8,128)} %param.19) | copy-start | bytes 196612
  33.0 3.0 %copy-start.3 = (f32[3,1024]{1,0:T(4,128)S(1)}, f32[3,1024]{1,0:T(4,128)}, u32[]{:S(2)}) copy-start(f32[3,1024]{1,0:T(4,128)} %param.20) | copy-start | bytes 36868
  33.0 3.0 %copy-start.5 = (f32[3,1024]{1,0:T(4,128)S(1)}, f32[3,1024]{1,0:T(4,128)}, u32[]{:S(2)}) copy-start(f32[3,1024]{1,0:T(4,128)} %param.21) | copy-start | bytes 36868
  33.5 2.6 %copy-start.8 = (s32[4]{0:T(128)S(1)}, s32[4]{0:T(128)}, u32[]{:S(2)}) copy-start(s32[4]{0:T(128)} %param.32) | copy-start | bytes 52
  109.7 120.0 %copy-start.2 = (f32[64,1024]{1,0:T(8,128)S(1)}, f32[64,1024]{1,0:T(8,128)}, u32[]{:S(2)}) copy-start(f32[64,1024]{1,0:T(8,128)} %param.23) | copy-start | bytes 786436
Sparse Core Ops, SparseCore 0:
  28.5 197.6 all-gather.2
where the time goes:
time: 239 us; the launch traced here: 237 us
  waiting for transfers between devices  116 us (49%)
  loops' own time  43.7 us (18%)
  matrix products  22 us (9%)
  local copies, waits for them, and re-layouts  20.9 us (9%)
  starting transfers between devices  16.3 us (7%)
  between operations  13.7 us (6%)
  other arithmetic  4.43 us (2%)
    all_gather x1, waiting for transfers between devices, on_device(): lax.all_gather(own_top.reshape(1, RHS * RANK), 'leaf', axis=0, tiled=True)  116 us
    another operation x1, loops' own time, on_device(): lax.map(one_leaf, (jnp.arange(leaf_count, dtype=jnp.int32), near_list, ne...  43.7 us
    dot_general x32, matrix products, block_term(): jnp.dot(lax.dynamic_slice_in_dim(wide_dens, start, LEAF, 1), block, preci...  18.1 us
    ppermute x2, starting transfers between devices, with_halo(): lax.ppermute(lax.slice_in_dim(block, 0, width, axis=dim), axis, backward)  11.2 us
    dynamic_slice x12, local copies, waits for them, and re-layouts, on_device(): lax.map(one_leaf, (jnp.arange(leaf_count, dtype=jnp.int32), near_list, ne...  7.88 us
    ppermute x2, starting transfers between devices, with_halo(): lax.ppermute(lax.slice_in_dim(block, block.shape[dim] - width, None, axis...  5.08 us
  transfers between devices with their start and end apart: 5, of which 1 were waited for; matrix products, arithmetic and copies ran while one was open for 17% of the time, Pallas kernels for 0%

commit v1 on v0

--- a/solution.py
+++ b/solution.py
@@ -110,7 +110,12 @@
     wide_normals = widened[RHS + 3 : RHS + 6]
     own_top = climb(own_mid, up_mid.reshape(1, 2, RANK, RANK))
     top_blocks = couple_top.reshape(1, ADM_TOP, RANK, RANK)
-    every_top = lax.all_gather(own_top.reshape(1, RHS * RANK), "leaf", axis=0, tiled=True)
+    every_top = jnp.concatenate(
+        lax.all_to_all(
+            jnp.stack([own_top.reshape(1, RHS * RANK)] * lax.axis_size("leaf")), "leaf", 0, 0
+        ),
+        axis=0,
+    )
     chosen_top = jnp.take(every_top, adm_top[0], axis=0).reshape(1, ADM_TOP, RHS, RANK)
     top_field = couple(chosen_top, top_blocks)
     mid_base = device_index * mid_count - mid_count

time: 239 us -> 158 us (0.66)
  waiting for transfers between devices: 116 us -> 0.01 us
  starting transfers between devices: 16.3 us -> 38.7 us
  local copies, waits for them, and re-layouts: 20.9 us -> 37.6 us
  between operations: 13.7 us -> 0.26 us
  other arithmetic: 4.43 us -> 9.62 us
  matrix products: 22 us -> 26.4 us
    all_gather x1 -> x0, waiting for transfers between devices: 116 us -> none  [on_device(): lax.all_gather(own_top.reshape(1, RHS * RANK), 'leaf', axis=0, tiled=True)]
    all_to_all x0 -> x1, starting transfers between devices: none -> 22.5 us  [on_device(): lax.all_to_all(jnp.stack([own_top.reshape(1, RHS * RANK)] * lax.axis_size...]
    another operation x3 -> x5, local copies, waits for them, and re-layouts: 1.19 us -> 6.05 us
    dynamic_slice x12, local copies, waits for them, and re-layouts: 7.88 us -> 10.6 us  [on_device(): lax.map(one_leaf, (jnp.arange(leaf_count, dtype=jnp.int32), near_list, ne...]
    dot_general x32, matrix products: 18.1 us -> 20.5 us  [block_term(): jnp.dot(lax.dynamic_slice_in_dim(wide_dens, start, LEAF, 1), block, preci...]
  transfers between devices with their start and end apart: 5 -> 5, of which waited for: 1 -> 0; matrix products, arithmetic and copies ran while one was open for 17% -> 41% of each run, Pallas kernels for 0% -> 0%
where the time goes in v1:
time: 158 us; the launch traced here: 156 us
  loops' own time  43.7 us (28%)
  starting transfers between devices  38.7 us (24%)
  local copies, waits for them, and re-layouts  37.6 us (24%)
  matrix products  26.4 us (17%)
  other arithmetic  9.62 us (6%)
    another operation x1, loops' own time, on_device(): lax.map(one_leaf, (jnp.arange(leaf_count, dtype=jnp.int32), near_list, ne...  43.7 us
    all_to_all x1, starting transfers between devices, on_device(): lax.all_to_all(jnp.stack([own_top.reshape(1, RHS * RANK)] * lax.axis_size...  22.5 us
    dot_general x32, matrix products, block_term(): jnp.dot(lax.dynamic_slice_in_dim(wide_dens, start, LEAF, 1), block, preci...  20.5 us
    ppermute x2, starting transfers between devices, with_halo(): lax.ppermute(lax.slice_in_dim(block, 0, width, axis=dim), axis, backward)  11.8 us
    dynamic_slice x12, local copies, waits for them, and re-layouts, on_device(): lax.map(one_leaf, (jnp.arange(leaf_count, dtype=jnp.int32), near_list, ne...  10.6 us
    ppermute x2, starting transfers between devices, with_halo(): lax.ppermute(lax.slice_in_dim(block, block.shape[dim] - width, None, axis...  4.49 us
    another operation x3, local copies, waits for them, and re-layouts  3.54 us
    dot_general x3, matrix products, couple(): return jnp.einsum('tark,takj->trj', sources, blocks, precision=highest)  3.53 us
  transfers between devices with their start and end apart: 5, of which 0 were waited for; matrix products, arithmetic and copies ran while one was open for 41% of the time, Pallas kernels for 0%

profile of v1, /device:TPU:1, one launch (start us, length us, event | category | flops | bytes accessed | tf_op | source)
XLA Modules:
  0.0 156.3 jit_solution(2329284801860301084)
XLA Ops:
  0.0 1.0 reshape.253
  1.0 1.3 fusion.193
  3.3 8.8 %collective-permute-start.3 = (f32[6,1024]{1,0:T(8,128)}, f32[6,1024]{1,0:T(8,128)}, u32[]{:S(2)}, u32[]{:S(2)}) collective-permute-start(f32[6,1024]{1,0:T(8,128)} %pad_maximum_fusion.5), channel_id=1, source_target_pairs={{1,0},{2,1},{3,2},{4,3},{5,4},{6,5},{7,6},{8,7},{9,8},{10,9},{11,1... | collective-permute-start | bytes 73736 | tf_op jit(solution)/shard_map/ppermute | solution.py:27
  12.1 1.9 %collective-permute-start.2 = (f32[6,1024]{1,0:T(8,128)}, f32[6,1024]{1,0:T(8,128)}, u32[]{:S(2)}, u32[]{:S(2)}) collective-permute-start(f32[6,1024]{1,0:T(8,128)} %pad_maximum_fusion.5), channel_id=1, source_target_pairs={{0,1},{1,2},{2,3},{3,4},{4,5},{5,6},{6,7},{7,8},{8,9},{9,10},{10,1... | collective-permute-start | bytes 73736 | tf_op jit(solution)/shard_map/ppermute | solution.py:24
  14.1 1.5 pad_maximum_fusion.1
  15.6 3.0 %collective-permute-start.1 = (f32[22,1024]{1,0:T(8,128)}, f32[22,1024]{1,0:T(8,128)}, u32[]{:S(2)}, u32[]{:S(2)}) collective-permute-start(f32[22,1024]{1,0:T(8,128)} %pad_maximum_fusion.1), channel_id=1, source_target_pairs={{1,0},{2,1},{3,2},{4,3},{5,4},{6,5},{7,6},{8,7},{9,8},{10,9},{11,1... | collective-permute-start | bytes 270344 | tf_op jit(solution)/shard_map/ppermute | solution.py:27
  18.6 2.6 %collective-permute-start = (f32[22,1024]{1,0:T(8,128)}, f32[22,1024]{1,0:T(8,128)}, u32[]{:S(2)}, u32[]{:S(2)}) collective-permute-start(f32[22,1024]{1,0:T(8,128)} %pad_maximum_fusion.1), channel_id=1, source_target_pairs={{0,1},{1,2},{2,3},{3,4},{4,5},{5,6},{6,7},{7,8},{8,9},{9,10},{10,1... | collective-permute-start | bytes 270344 | tf_op jit(solution)/shard_map/ppermute | solution.py:24
  21.1 0.9 reshape.262
  22.3 2.4 %stack.3 = f32[512,1,1024]{2,1,0:T(1,128)} broadcast(f32[1024]{0:T(1024)S(1)} %stack_reshape.2), dimensions={2} | broadcast | bytes 2101248 | tf_op jit(solution)/shard_map/stack | solution.py:115
  24.8 22.5 %all-to-all-start = ((f32[512,1,1024]{2,1,0:T(1,128)}), f32[512,1,1024]{2,1,0:T(1,128)S(1)}, u32[]{:S(2)}, u32[]{:S(2)}) async-start(f32[512,1,1024]{2,1,0:T(1,128)} %stack.3), calls=%async_computation | async-start | bytes 4194304 | tf_op jit(solution)/shard_map/all_to_all | solution.py:114
  51.3 1.0 reshape.260
  52.4 1.2 reshape.264
  53.6 1.5 reshape.265
  55.0 1.6 %reshape.267 = f32[2,2,64,64]{3,2,1,0:T(8,128)} reshape(f32[4,4096]{1,0:T(4,128)} %param.26) | data formatting | bytes 131072 | tf_op jit(solution)/shard_map/reshape | solution.py:128
  56.7 1.4 pad_maximum_fusion.2
  58.1 1.6 %reshape.255 = f32[3,6,16,64]{3,2,1,0:T(8,128)} reshape(f32[18,1024]{1,0:T(8,128)} %pad_maximum_fusion.2) | data formatting | bytes 147456 | tf_op jit(solution)/shard_map/reshape | solution.py:105
  59.8 1.5 slice.233
  61.3 0.8 slice.234
  62.1 2.2 %gather_fusion = f32[24,16,64]{2,1,0:T(8,128)} fusion(f32[12,16,64]{2,1,0:T(8,128)} %bitcast.294, s32[1024]{0:T(1024)} %pad_clamp_fusion.2), kind=kCustom, calls=%fused_computation | custom fusion | bytes 196704 | tf_op jit(solution)/shard_map/jit(_take)/gather | solution.py:126
  64.3 1.3 gather_fusion.1
  65.7 1.6 %fusion.188 = f32[4,16,64,1]{2,1,3,0:T(8,128)S(1)} fusion(f32[4,6,64,64]{3,2,0,1:T(8,128)S(1)} %reshape.257, f32[4,6,16,64]{3,2,1,0:T(8,128)} %bitcast.295, pred[4,6]{1,0:T(4,128)(4,1)} %get-tuple-element.80), kind=kOutput, calls=%fused_computation.264 | convolution fusion | flops 18898944 | bytes 507928 | tf_op jit(solution)/shard_map/tark,takj->trj/dot_general | solution.py:70
  67.3 1.5 convolution_bitcast_fusion.4
  68.9 1.0 pad_maximum_fusion
  69.9 0.9 pad_maximum_fusion.3
  70.7 78.8 %while.10 = (s32[]{:T(128)}, f32[4,16,256]{2,1,0:T(8,128)}, s32[4]{0:T(128)}, s32[4,8]{1,0:T(4,128)}, s32[]{:T(128)}, /*index=5*/f32[16,3072]{1,0:T(8,128)S(1)},...) while((s32[]{:T(128)}, f32[4,16,256]{2,1,0:T(8,128)}, ...), condition=%wide.region_1.2_spmd, body=%wide.region_0.1_spmd.sunk | while | flops 109637680 | bytes 556646 | solution.py:153
  70.7 0.7 constant_dynamic-slice_fusion.21
  71.4 0.7 fusion.260
  77.3 0.7 dynamic_slice.123
  78.8 1.3 dynamic_slice.124
  89.3 1.2 fusion.267
  90.4 0.7 constant_dynamic-slice_fusion.21
  91.1 0.7 fusion.260
  97.0 0.7 dynamic_slice.123
  98.4 1.3 dynamic_slice.124
  108.9 1.2 fusion.267
  110.1 0.7 constant_dynamic-slice_fusion.21
  110.8 0.7 fusion.260
  116.7 0.7 dynamic_slice.123
  118.1 1.3 dynamic_slice.124
  128.6 1.2 fusion.267
  129.8 0.7 constant_dynamic-slice_fusion.21
  130.5 0.7 fusion.260
  136.3 0.7 dynamic_slice.123
  137.8 1.3 dynamic_slice.124
  148.3 1.2 fusion.267
  149.5 0.8 copy.46
  150.4 1.8 %copy.65 = f32[512,1,1024]{2,0,1:T(8,128)} copy(f32[512,1,1024]{2,1,0:T(1,128)S(1)} %all-to-all-done) | data formatting | bytes 4194304
  152.2 2.3 %gather_fusion.2 = f32[16,1024]{1,0:T(8,128)S(1)} fusion(f32[512,1024]{1,0:T(8,128)} %bitcast.292, s32[1024]{0:T(1024)} %pad_clamp_fusion), kind=kCustom, calls=%fused_computation.2 | custom fusion | bytes 131136 | tf_op jit(solution)/shard_map/jit(_take)/gather | solution.py:119
  (92 shorter events, 24.3 us)
Async XLA Ops:
  3.3 53.3 %collective-permute-start.3 = (f32[6,1024]{1,0:T(8,128)}, f32[6,1024]{1,0:T(8,128)}, u32[]{:S(2)}, u32[]{:S(2)}) collective-permute-start(f32[6,1024]{1,0:T(8,128)} %pad_maximum_fusion.5), channel_id=1, source_target_pairs={{1,0},{2,1},{3,2},{4,3},{5,4},{6,5},{7,6},{8,7},{9,8},{10,9},{11,1... | collective-permute-start | bytes 73736 | tf_op jit(solution)/shard_map/ppermute | solution.py:27
  12.1 44.6 %collective-permute-start.2 = (f32[6,1024]{1,0:T(8,128)}, f32[6,1024]{1,0:T(8,128)}, u32[]{:S(2)}, u32[]{:S(2)}) collective-permute-start(f32[6,1024]{1,0:T(8,128)} %pad_maximum_fusion.5), channel_id=1, source_target_pairs={{0,1},{1,2},{2,3},{3,4},{4,5},{5,6},{6,7},{7,8},{8,9},{9,10},{10,1... | collective-permute-start | bytes 73736 | tf_op jit(solution)/shard_map/ppermute | solution.py:24
  15.6 53.2 %collective-permute-start.1 = (f32[22,1024]{1,0:T(8,128)}, f32[22,1024]{1,0:T(8,128)}, u32[]{:S(2)}, u32[]{:S(2)}) collective-permute-start(f32[22,1024]{1,0:T(8,128)} %pad_maximum_fusion.1), channel_id=1, source_target_pairs={{1,0},{2,1},{3,2},{4,3},{5,4},{6,5},{7,6},{8,7},{9,8},{10,9},{11,1... | collective-permute-start | bytes 270344 | tf_op jit(solution)/shard_map/ppermute | solution.py:27
  18.6 50.2 %collective-permute-start = (f32[22,1024]{1,0:T(8,128)}, f32[22,1024]{1,0:T(8,128)}, u32[]{:S(2)}, u32[]{:S(2)}) collective-permute-start(f32[22,1024]{1,0:T(8,128)} %pad_maximum_fusion.1), channel_id=1, source_target_pairs={{0,1},{1,2},{2,3},{3,4},{4,5},{5,6},{6,7},{7,8},{8,9},{9,10},{10,1... | collective-permute-start | bytes 270344 | tf_op jit(solution)/shard_map/ppermute | solution.py:24
  24.7 22.5 %copy-start.11 = (s32[1,16]{1,0:T(1,128)S(1)}, s32[1,16]{1,0:T(1,128)}, u32[]{:S(2)}) copy-start(s32[1,16]{1,0:T(1,128)} %param.35) | copy-start | bytes 196
  24.7 23.1 %copy-start.8 = (s32[4,6]{1,0:T(4,128)S(1)}, s32[4,6]{1,0:T(4,128)}, u32[]{:S(2)}) copy-start(s32[4,6]{1,0:T(4,128)} %param.33) | copy-start | bytes 292
  24.7 24.3 %copy-start.9 = (s32[2,6]{1,0:T(2,128)S(1)}, s32[2,6]{1,0:T(2,128)}, u32[]{:S(2)}) copy-start(s32[2,6]{1,0:T(2,128)} %param.34) | copy-start | bytes 148
  24.7 26.2 %copy-start.2 = (f32[4,6,4096]{2,0,1:T(4,128)S(1)}, f32[4,6,4096]{2,0,1:T(4,128)}, u32[]{:S(2)}) copy-start(f32[4,6,4096]{2,0,1:T(4,128)} %param.28) | copy-start | bytes 1179652
  24.7 26.6 %copy-start.6 = (f32[2,6,4096]{2,0,1:T(2,128)S(1)}, f32[2,6,4096]{2,0,1:T(2,128)}, u32[]{:S(2)}) copy-start(f32[2,6,4096]{2,0,1:T(2,128)} %param.29) | copy-start | bytes 589828
  24.8 125.6 %all-to-all-start = ((f32[512,1,1024]{2,1,0:T(1,128)}), f32[512,1,1024]{2,1,0:T(1,128)S(1)}, u32[]{:S(2)}, u32[]{:S(2)}) async-start(f32[512,1,1024]{2,1,0:T(1,128)} %stack.3), calls=%async_computation | async-start | bytes 4194304 | tf_op jit(solution)/shard_map/all_to_all | solution.py:114
  52.4 16.5 %copy-start = (f32[16,1024]{1,0:T(8,128)S(1)}, f32[16,1024]{1,0:T(8,128)}, u32[]{:S(2)}) copy-start(f32[16,1024]{1,0:T(8,128)} %param.19) | copy-start | bytes 196612
  52.4 16.5 %copy-start.5 = (f32[3,1024]{1,0:T(4,128)S(1)}, f32[3,1024]{1,0:T(4,128)}, u32[]{:S(2)}) copy-start(f32[3,1024]{1,0:T(4,128)} %param.20) | copy-start | bytes 36868
  52.4 16.5 %copy-start.7 = (f32[3,1024]{1,0:T(4,128)S(1)}, f32[3,1024]{1,0:T(4,128)}, u32[]{:S(2)}) copy-start(f32[3,1024]{1,0:T(4,128)} %param.21) | copy-start | bytes 36868
  150.3 4.2 %copy-start.10 = (pred[16]{0:T(512)(128)(4,1)S(1)}, pred[16]{0:T(512)(128)(4,1)}, u32[]{:S(2)}) copy-start(pred[16]{0:T(512)(128)(4,1)} %compare_and_fusion) | copy-start | bytes 52
  150.3 4.7 %copy-start.4 = (f32[2,64,64]{2,1,0:T(8,128)S(1)}, f32[2,64,64]{2,1,0:T(8,128)}, u32[]{:S(2)}) copy-start(f32[2,64,64]{2,1,0:T(8,128)} %reshape.265) | copy-start | bytes 98308
  150.3 4.9 %copy-start.1 = (f32[2,2,64,64]{3,2,1,0:T(8,128)S(1)}, f32[2,2,64,64]{3,2,1,0:T(8,128)}, u32[]{:S(2)}) copy-start(f32[2,2,64,64]{3,2,1,0:T(8,128)} %reshape.267) | copy-start | bytes 196612
  150.3 5.1 %copy-start.3 = (f32[64,1024]{1,0:T(8,128)S(1)}, f32[64,1024]{1,0:T(8,128)}, u32[]{:S(2)}) copy-start(f32[64,1024]{1,0:T(8,128)} %param.23) | copy-start | bytes 786436
